TPU v7x, 32 devices: a whole 2x2x4 slice. The times are simulated.
32 devices in a mesh: groups: 2 (over x), leaf: 16 (over z, y, core).
Axes of the slice: x: 2, y: 2, z: 4, core: 2. Of those that a mesh axis runs over, the one named last changes fastest.
Arguments:
- right_side: float32 [256, 65536], P('groups', 'leaf'), parts along dimension 0, may hold values from -30 to 30
- point_order: int32 [131072], P(('groups', 'leaf')), parts along dimension 0, may hold values from 0 to 65535, as said below
- leaf_blocks: bfloat16 [128, 512, 512], P('leaf'), may hold values from -0.01 to 6, as said below
- bases: bfloat16 [7, 128, 65536], P(None, None, 'leaf'), may hold values from -4 to 4
- rank_weights: float32 [7, 128], replicated, may hold values from 0.05 to 0.6
Outputs:
- field_solution: float32 [256, 65536], P('groups', 'leaf'), parts along dimension 0
- field_residual: float32 [256, 65536], P('groups', 'leaf'), parts along dimension 0
There are 2 independent parts, one for each index of `groups`. A program takes and returns all parts, laid end to end along the dimension named above; an argument that names none is the same for every part. Nothing has to cross between parts.
Inputs may be any that keep to these rules, and one draw needn't show every extreme that they name: `point_order`: each aligned run of 4096 entries holds each of its own 4096 positions once. `leaf_blocks`: every block is symmetric positive definite.
All inputs are finite; a program needn't handle non-finite values.
Results may differ from a plain program's by a relative error of at most 0.0049.
Values sent between devices are 32-bit elements; how exact they have to be, the bound alone decides.
A program may use at most 128 MiB of HBM per device.

v0:
```python
import math
import jax
import jax.numpy as jnp
from jax import lax
from jax.sharding import PartitionSpec as P

ITERS = 2


def from_partner(array, axis, stride):
    return lax.ppermute(array, axis, [(i, i ^ 1 << stride) for i in range(lax.axis_size(axis))])


def scale_level(values, tree_level, rank_weights, leaf_size):
    rank_size = rank_weights.shape[1]
    factor = 1.0 / math.sqrt(rank_size * leaf_size * 2 ** (tree_level + 1))
    return (values * factor * rank_weights[tree_level]).astype(jnp.bfloat16)


def double_up(stacked):
    finished = []
    pending = stacked
    for tree_bit in range(stacked.shape[0]):
        received = from_partner(pending, "leaf", tree_bit)
        pending = pending + received
        finished.append(pending[0])
        pending = pending[1:]
    return finished


def apply_operator(probe, leaf_blocks, bases, rank_weights):
    columns, points = probe.shape
    blocks, leaf_size = (leaf_blocks.shape[0], leaf_blocks.shape[1])
    levels, rank_size = rank_weights.shape
    upper_levels = lax.axis_size("leaf").bit_length() - 1
    local_levels = levels - upper_levels
    probe_tiles = probe.reshape(columns, blocks, leaf_size)
    basis_tiles = bases.reshape(levels, rank_size, blocks, leaf_size)
    dense_part = jnp.einsum(
        "nbj,bjp->nbp", probe_tiles, leaf_blocks, preferred_element_type=jnp.float32
    )
    partial_value = jnp.einsum(
        "nbp,lrbp->blnr", probe_tiles, basis_tiles, preferred_element_type=jnp.float32
    )
    scaled_levels = []
    for tree_level in range(local_levels):
        per_node = 2 ** (tree_level + 1)
        grouped = (
            partial_value[:, tree_level]
            .reshape(blocks // per_node, per_node, columns, rank_size)
            .sum(axis=1)
        )
        scaled = scale_level(grouped, tree_level, rank_weights, leaf_size)
        scaled_levels.append(jnp.repeat(scaled, per_node, axis=0))
    device_terms = partial_value[:, local_levels:].sum(axis=0)
    level_totals = double_up(device_terms)
    for offset_level, level_total in enumerate(level_totals):
        scaled = scale_level(level_total, local_levels + offset_level, rank_weights, leaf_size)
        scaled_levels.append(jnp.broadcast_to(scaled, (blocks, columns, rank_size)))
    stacked = jnp.stack(scaled_levels)
    low_rank = jnp.einsum(
        "lbnr,lrbp->nbp", stacked, basis_tiles, preferred_element_type=jnp.float32
    )
    return (dense_part + low_rank).reshape(columns, points)


def squares(values):
    return lax.psum(jnp.sum(values * values, axis=1), "leaf")


def on_device(right_side, point_order, leaf_blocks, bases, rank_weights):
    columns, points = right_side.shape
    first_point = lax.axis_index("leaf") * points
    local_order = point_order - first_point
    ordered = jnp.take(right_side, local_order, axis=1)
    solution = jnp.zeros_like(ordered)
    residual = ordered
    direction = ordered
    norm_now = squares(residual)
    for iteration in range(ITERS):
        image_field = apply_operator(
            direction.astype(jnp.bfloat16), leaf_blocks, bases, rank_weights
        )
        curvature = lax.psum(jnp.sum(direction * image_field, axis=1), "leaf")
        step_size = norm_now / curvature
        solution = solution + step_size[:, None] * direction
        residual = residual - step_size[:, None] * image_field
        if iteration + 1 < ITERS:
            norm_next = squares(residual)
            direction = residual + (norm_next / norm_now)[:, None] * direction
            norm_now = norm_next
    field_solution = jnp.zeros_like(solution).at[:, local_order].set(solution)
    field_residual = jnp.zeros_like(residual).at[:, local_order].set(residual)
    return (field_solution, field_residual)


def solution(mesh):
    return jax.shard_map(
        on_device,
        mesh=mesh,
        in_specs=(
            P("groups", "leaf"),
            P(("groups", "leaf")),
            P("leaf", None, None),
            P(None, None, "leaf"),
            P(),
        ),
        out_specs=(P("groups", "leaf"), P("groups", "leaf")),
        check_vma=False,
    )
```

profile of v0, /device:TPU:0, one launch (start us, length us, event | category | flops | bytes accessed | tf_op | source)
XLA Modules:
  0.0 227.0 jit_solution(16715418856772773228)
XLA Ops:
  0.6 0.7 compare_and_fusion
  1.4 1.9 copy.14
  3.3 14.2 %gather_fusion = f32[4096,128]{1,0:T(8,128)} fusion(f32[128,4096]{0,1:T(8,128)S(1)} %copy.14, s32[4096]{0:T(1024)S(1)} %broadcast_clamp_fusion), kind=kCustom, calls=%fused_computation | custom fusion | bytes 4210688 | tf_op jit(solution)/shard_map/jit(_take)/gather | solution.py:75
  17.5 1.9 copy.15
  19.4 5.5 %fusion.25 = f32[8,7,128,128]{3,2,1,0:T(8,128)S(1)} fusion(bf16[7,16,8,8,512]{4,3,2,1,0:T(8,128)(2,1)} %bitcast.155, f32[128,8,512]{2,0,1:T(8,128)S(1)} %copy.15, pred[8,512]{1,0:T(8,128)(4,1)S(1)} %broadcast_in_dim.46), kind=kOutput, calls=%fused_computation.41 | convolution fusion | flops 940048384 | bytes 13111296 | tf_op jit(solution)/shard_map/nbp,lrbp->blnr/dot_general | solution.py:42
  25.0 0.1 slice_reduce_fusion.1
  25.1 0.5 collective-permute-start
  25.6 0.1 slice_reduce_fusion.3
  25.7 0.8 copy-done
  26.6 2.1 multiply_reduce_fusion.3
  28.9 0.8 fusion.47
  30.1 3.0 %collective-permute-start.1 = (f32[3,128,128]{2,1,0:T(8,128)S(1)}, f32[3,128,128]{2,1,0:T(8,128)S(1)}, u32[]{:S(2)}, u32[]{:S(2)}) collective-permute-start(f32[3,128,128]{2,1,0:T(8,128)S(1)} %slice.122), channel_id=1, source_target_pairs={{0,2},{1,3},{2,0},{3,1},{4,6},{5,7},{6,4},{7,5},{8,10},{9,11},{10,... | collective-permute-start | bytes 589832 | tf_op jit(solution)/shard_map/ppermute | solution.py:11
  33.2 4.8 %collective-permute-done.1 = f32[3,128,128]{2,1,0:T(8,128)S(1)} collective-permute-done((f32[3,128,128]{2,1,0:T(8,128)S(1)}, f32[3,128,128]{2,1,0:T(8,128)S(1)}, u32[]{:S(2)}, u32[]{:S(2)}) %collective-permute-start.1) | collective-permute-done | bytes 196640 | tf_op jit(solution)/shard_map/ppermute | solution.py:11
  38.0 1.9 collective-permute-start.2
  39.9 3.2 %collective-permute-done.2 = f32[2,128,128]{2,1,0:T(8,128)S(1)} collective-permute-done((f32[2,128,128]{2,1,0:T(8,128)S(1)}, f32[2,128,128]{2,1,0:T(8,128)S(1)}, u32[]{:S(2)}, u32[]{:S(2)}) %collective-permute-start.2) | collective-permute-done | bytes 131104 | tf_op jit(solution)/shard_map/ppermute | solution.py:11
  43.1 2.9 %collective-permute-start.3 = (f32[1,128,128]{2,1,0:T(8,128)S(1)}, f32[1,128,128]{2,1,0:T(8,128)S(1)}, u32[]{:S(2)}, u32[]{:S(2)}) collective-permute-start(f32[1,128,128]{2,1,0:T(8,128)S(1)} %slice.126), channel_id=1, source_target_pairs={{0,8},{1,9},{2,10},{3,11},{4,12},{5,13},{6,14},{7,15},{8,0},{9,1},... | collective-permute-start | bytes 196616 | tf_op jit(solution)/shard_map/ppermute | solution.py:11
  46.0 2.3 %collective-permute-done.3 = f32[1,128,128]{2,1,0:T(8,128)S(1)} collective-permute-done((f32[1,128,128]{2,1,0:T(8,128)S(1)}, f32[1,128,128]{2,1,0:T(8,128)S(1)}, u32[]{:S(2)}, u32[]{:S(2)}) %collective-permute-start.3) | collective-permute-done | bytes 65568 | tf_op jit(solution)/shard_map/ppermute | solution.py:11
  48.5 2.8 %multiply_reduce_fusion.2 = (f32[128]{0:T(128)S(1)}, f32[128,8,512]{2,0,1:T(8,128)}) fusion(f32[128,8,512]{2,0,1:T(8,128)S(1)} %copy.15, pred[8,512]{1,0:T(8,128)(4,1)S(1)} %broadcast_in_dim.46, f32[8,128,512]{2,1,0:T(8,128)S(1)} %fusion.47, bf16[7,8,128,128]{3,2,0,1:T(8,128)(2,1)S(1)} %broadcast_dynamic-update-slice_fusion.5, ...), kind=kOutput, calls=%fused_computation.39 | convolution fusion | flops 941621120 | bytes 15471104 | tf_op jit(solution)/shard_map/lbnr,lrbp->nbp/dot_general | solution.py:61
  51.3 31.1 %all-reduce = (f32[128]{0:T(128)S(1)}, f32[128]{0:T(128)S(1)}) all-reduce(f32[128]{0:T(128)S(1)} %multiply_reduce_fusion.3, f32[128]{0:T(128)S(1)} %get-tuple-element.29), channel_id=1, replica_groups=mesh['groups'=2,'leaf'=16] {'leaf'}, use_global_device_ids=true, to_apply=%region_1.2 | all-reduce | flops 256 | bytes 2048 | tf_op jit(solution)/shard_map/psum | solution.py:68
  82.4 2.1 multiply_reduce_fusion.1
  84.5 29.7 %psum.30 = f32[128]{0:T(128)S(1)} all-reduce(f32[128]{0:T(128)S(1)} %multiply_reduce_fusion.1), channel_id=1, replica_groups=mesh['groups'=2,'leaf'=16] {'leaf'}, use_global_device_ids=true, to_apply=%region_9.10 | all-reduce | flops 128 | bytes 1024 | tf_op jit(solution)/shard_map/psum | solution.py:68
  114.2 2.2 multiply_add_fusion
  116.4 6.3 %fusion.28 = f32[8,7,128,128]{3,2,1,0:T(8,128)S(1)} fusion(bf16[7,16,8,8,512]{4,3,2,1,0:T(8,128)(2,1)} %bitcast.156, f32[128,8,512]{2,0,1:T(8,128)S(1)} %multiply_add_fusion), kind=kOutput, calls=%fused_computation.42 | convolution fusion | flops 940048384 | bytes 13107200 | tf_op jit(solution)/shard_map/nbp,lrbp->blnr/dot_general | solution.py:42
  122.7 0.1 slice_reduce_fusion
  122.8 0.1 slice_reduce_fusion.2
  122.9 2.0 copy-done.6
  124.8 2.0 fusion.45
  127.0 0.7 constant_dynamic-update-slice_fusion.3
  127.9 0.8 constant_dynamic-update-slice_fusion.2
  128.6 1.8 copy.20
  130.5 0.7 broadcast_dynamic-update-slice_fusion.4
  131.4 0.7 broadcast_dynamic-update-slice_fusion.3
  132.1 6.6 %collective-permute-done.5 = f32[3,128,128]{2,1,0:T(8,128)S(1)} collective-permute-done((f32[3,128,128]{2,1,0:T(8,128)S(1)}, f32[3,128,128]{2,1,0:T(8,128)S(1)}, u32[]{:S(2)}, u32[]{:S(2)}) %collective-permute-start.5) | collective-permute-done | bytes 196640 | tf_op jit(solution)/shard_map/ppermute | solution.py:11
  138.7 0.1 collective-permute-start.6
  138.8 5.1 %collective-permute-done.6 = f32[2,128,128]{2,1,0:T(8,128)S(1)} collective-permute-done((f32[2,128,128]{2,1,0:T(8,128)S(1)}, f32[2,128,128]{2,1,0:T(8,128)S(1)}, u32[]{:S(2)}, u32[]{:S(2)}) %collective-permute-start.6) | collective-permute-done | bytes 131104 | tf_op jit(solution)/shard_map/ppermute | solution.py:11
  143.9 0.1 collective-permute-start.7
  144.0 0.7 broadcast_dynamic-update-slice_fusion.2
  144.8 4.8 %collective-permute-done.7 = f32[1,128,128]{2,1,0:T(8,128)S(1)} collective-permute-done((f32[1,128,128]{2,1,0:T(8,128)S(1)}, f32[1,128,128]{2,1,0:T(8,128)S(1)}, u32[]{:S(2)}, u32[]{:S(2)}) %collective-permute-start.7) | collective-permute-done | bytes 65568 | tf_op jit(solution)/shard_map/ppermute | solution.py:11
  149.6 0.7 broadcast_dynamic-update-slice_fusion.1
  150.3 0.7 broadcast_dynamic-update-slice_fusion
  151.1 6.4 %multiply_reduce_fusion = (f32[128]{0:T(128)S(1)}, f32[128,8,512]{2,0,1:T(8,128)}) fusion(f32[128,8,512]{2,0,1:T(8,128)S(1)} %copy-done.3, f32[8,128,512]{2,1,0:T(8,128)S(1)} %copy-done.7, bf16[7,8,128,128]{3,2,0,1:T(8,128)(2,1)} %broadcast_dynamic-update-slice_fusion, bf16[7,16,8,8,512]{4,3,2,1,0:T(8,128)(2,1)} %bitcast.157), kind=kOutput, calls=%fused_computation.34 | convolution fusion | flops 941096832 | bytes 15467008 | tf_op jit(solution)/shard_map/lbnr,lrbp->nbp/dot_general | solution.py:61
  157.4 29.5 %psum.31 = f32[128]{0:T(128)S(1)} all-reduce(f32[128]{0:T(128)S(1)} %get-tuple-element.31), channel_id=1, replica_groups=mesh['groups'=2,'leaf'=16] {'leaf'}, use_global_device_ids=true, to_apply=%region_15.16 | all-reduce | flops 128 | bytes 1024 | tf_op jit(solution)/shard_map/psum | solution.py:84
  186.9 3.1 %copy.21 = f32[128,8,512]{0,2,1:T(8,128)} copy(f32[128,8,512]{2,0,1:T(8,128)} %get-tuple-element.32) | data formatting | bytes 4194304 | tf_op jit(solution)/shard_map/add | solution.py:64
  190.0 3.9 %fusion.14 = (f32[128,4096]{0,1:T(8,128)}, f32[128,4096]{0,1:T(8,128)}) fusion(f32[128,8,512]{0,2,1:T(8,128)} %copy.21, f32[128]{0:T(128)S(1)} %div.11, f32[128,8,512]{0,2,1:T(8,128)} %copy.20, f32[128]{0:T(128)S(1)} %div.9, f32[4096,128]{1,0:T(8,128)S(1)} %copy-done.1, pred[4096]{0:T(1024)(128)(4,1)S(1)} %get-tuple-element.10), kind=kLoop, calls=%fused_computation.20 | loop fusion | flops 2621440 | bytes 10490880 | tf_op jit(solution)/shard_map/sub | solution.py:87
  193.9 12.5 %scatter_custom_fusion.1 = f32[128,4096]{0,1:T(8,128)} fusion(s32[4096]{0:T(1024)S(1)} %get-tuple-element.11, f32[128,4096]{0,1:T(8,128)} %get-tuple-element.8, f32[]{:T(128)} %constant.13.clone.1), kind=kCustom, calls=%fused_computation.17 | custom fusion | bytes 4194308 | tf_op jit(solution)/shard_map/scatter | solution.py:93
  206.4 2.9 %copy.23 = f32[128,4096]{1,0:T(8,128)} copy(f32[128,4096]{0,1:T(8,128)} %scatter_custom_fusion.1) | data formatting | bytes 4194304
  209.3 14.8 %scatter_custom_fusion = f32[128,4096]{0,1:T(8,128)} fusion(s32[4096]{0:T(1024)S(1)} %get-tuple-element.11, f32[128,4096]{0,1:T(8,128)} %get-tuple-element.9, f32[4096,128]{1,0:T(8,128)S(1)} %copy-done.1, f32[128]{0:T(128)S(1)} %div.10, f32[128]{0:T(128)S(1)} %div.11, f32[128]{0:T(128)S(1)} %div.9, f32[]{:T(128)} %constant.18.clone.1, ...), kind=kCustom, calls=%fused_computation.21 | custom fusion | flops 3145728 | bytes 6297096 | tf_op jit(solution)/shard_map/scatter | solution.py:92
  224.1 2.9 %copy.22 = f32[128,4096]{1,0:T(8,128)} copy(f32[128,4096]{0,1:T(8,128)} %scatter_custom_fusion) | data formatting | bytes 4194304
  (70 shorter events, 1.2 us)
Async XLA Ops:
  25.0 1.6 copy-start
  25.1 3.6 %copy-start.8 = (f32[7,128]{1,0:T(8,128)S(1)}, f32[7,128]{1,0:T(8,128)}, u32[]{:S(2)}) copy-start(f32[7,128]{1,0:T(8,128)} %param.9) | copy-start | bytes 10756
  25.1 4.9 %collective-permute-start = (f32[4,128,128]{2,1,0:T(8,128)S(1)}, f32[4,128,128]{2,1,0:T(8,128)S(1)}, u32[]{:S(2)}, u32[]{:S(2)}) collective-permute-start(f32[4,128,128]{2,1,0:T(8,128)S(1)} %slice_reduce_fusion.1), channel_id=1, source_target_pairs={{0,1},{1,0},{2,3},{3,2},{4,5},{5,4},{6,7},{7,6},{8,9},{9,8},{10,11... | collective-permute-start | bytes 786440 | tf_op jit(solution)/shard_map/ppermute | solution.py:11
  26.6 2.4 %copy-start.5 = (bf16[8,512,512]{2,1,0:T(8,128)(2,1)S(1)}, bf16[8,512,512]{2,1,0:T(8,128)(2,1)}, u32[]{:S(2)}) copy-start(bf16[8,512,512]{2,1,0:T(8,128)(2,1)} %param.7) | copy-start | bytes 12582916
  28.9 19.6 %slice-start = ((s8[7340032]{0:T(1024)(128)(4,1)}), s8[4194304]{0:T(1024)(128)(4,1)S(1)}, s32[]{:S(2)}) async-start(s8[7340032]{0:T(1024)(128)(4,1)} %bitcast.158), calls=%async_computation | async-start | bytes 8388608
  28.9 19.6 %slice-start.1 = ((s8[7340032]{0:T(1024)(128)(4,1)}), s8[3145728]{0:T(1024)(128)(4,1)S(1)}, s32[]{:S(2)}) async-start(s8[7340032]{0:T(1024)(128)(4,1)} %bitcast.158), calls=%async_computation.1 | async-start | bytes 6291456
  30.1 7.9 %collective-permute-start.1 = (f32[3,128,128]{2,1,0:T(8,128)S(1)}, f32[3,128,128]{2,1,0:T(8,128)S(1)}, u32[]{:S(2)}, u32[]{:S(2)}) collective-permute-start(f32[3,128,128]{2,1,0:T(8,128)S(1)} %slice.122), channel_id=1, source_target_pairs={{0,2},{1,3},{2,0},{3,1},{4,6},{5,7},{6,4},{7,5},{8,10},{9,11},{10,... | collective-permute-start | bytes 589832 | tf_op jit(solution)/shard_map/ppermute | solution.py:11
  38.0 5.0 %collective-permute-start.2 = (f32[2,128,128]{2,1,0:T(8,128)S(1)}, f32[2,128,128]{2,1,0:T(8,128)S(1)}, u32[]{:S(2)}, u32[]{:S(2)}) collective-permute-start(f32[2,128,128]{2,1,0:T(8,128)S(1)} %slice.124), channel_id=1, source_target_pairs={{0,4},{1,5},{2,6},{3,7},{4,0},{5,1},{6,2},{7,3},{8,12},{9,13},{10,... | collective-permute-start | bytes 393224 | tf_op jit(solution)/shard_map/ppermute | solution.py:11
  43.1 5.2 %collective-permute-start.3 = (f32[1,128,128]{2,1,0:T(8,128)S(1)}, f32[1,128,128]{2,1,0:T(8,128)S(1)}, u32[]{:S(2)}, u32[]{:S(2)}) collective-permute-start(f32[1,128,128]{2,1,0:T(8,128)S(1)} %slice.126), channel_id=1, source_target_pairs={{0,8},{1,9},{2,10},{3,11},{4,12},{5,13},{6,14},{7,15},{8,0},{9,1},... | collective-permute-start | bytes 196616 | tf_op jit(solution)/shard_map/ppermute | solution.py:11
  116.4 6.5 %copy-start.2 = (f32[128,8,512]{2,0,1:T(8,128)}, f32[128,8,512]{2,0,1:T(8,128)S(1)}, u32[]{:S(2)}) copy-start(f32[128,8,512]{2,0,1:T(8,128)S(1)} %multiply_add_fusion) | copy-start | bytes 6291460
  122.7 2.2 copy-start.6
  126.9 1.7 copy-start.4
  126.9 4.3 %collective-permute-start.4 = (f32[4,128,128]{2,1,0:T(8,128)S(1)}, f32[4,128,128]{2,1,0:T(8,128)S(1)}, u32[]{:S(2)}, u32[]{:S(2)}) collective-permute-start(f32[4,128,128]{2,1,0:T(8,128)S(1)} %slice_reduce_fusion), channel_id=1, source_target_pairs={{0,1},{1,0},{2,3},{3,2},{4,5},{5,4},{6,7},{7,6},{8,9},{9,8},{10,11... | collective-permute-start | bytes 786440 | tf_op jit(solution)/shard_map/ppermute | solution.py:11
  131.2 19.9 %copy-start.3 = (f32[128,8,512]{2,0,1:T(8,128)S(1)}, f32[128,8,512]{2,0,1:T(8,128)}, u32[]{:S(2)}) copy-start(f32[128,8,512]{2,0,1:T(8,128)} %copy-done.2) | copy-start | bytes 6291460
  131.2 19.9 %copy-start.7 = (f32[8,128,512]{2,1,0:T(8,128)S(1)}, f32[8,128,512]{2,1,0:T(8,128)}, u32[]{:S(2)}) copy-start(f32[8,128,512]{2,1,0:T(8,128)} %fusion.45) | copy-start | bytes 6291460
  131.3 7.4 %collective-permute-start.5 = (f32[3,128,128]{2,1,0:T(8,128)S(1)}, f32[3,128,128]{2,1,0:T(8,128)S(1)}, u32[]{:S(2)}, u32[]{:S(2)}) collective-permute-start(f32[3,128,128]{2,1,0:T(8,128)S(1)} %slice.132), channel_id=1, source_target_pairs={{0,2},{1,3},{2,0},{3,1},{4,6},{5,7},{6,4},{7,5},{8,10},{9,11},{10,... | collective-permute-start | bytes 589832 | tf_op jit(solution)/shard_map/ppermute | solution.py:11
  138.7 5.2 %collective-permute-start.6 = (f32[2,128,128]{2,1,0:T(8,128)S(1)}, f32[2,128,128]{2,1,0:T(8,128)S(1)}, u32[]{:S(2)}, u32[]{:S(2)}) collective-permute-start(f32[2,128,128]{2,1,0:T(8,128)S(1)} %slice.134), channel_id=1, source_target_pairs={{0,4},{1,5},{2,6},{3,7},{4,0},{5,1},{6,2},{7,3},{8,12},{9,13},{10,... | collective-permute-start | bytes 393224 | tf_op jit(solution)/shard_map/ppermute | solution.py:11
  143.9 5.7 %collective-permute-start.7 = (f32[1,128,128]{2,1,0:T(8,128)S(1)}, f32[1,128,128]{2,1,0:T(8,128)S(1)}, u32[]{:S(2)}, u32[]{:S(2)}) collective-permute-start(f32[1,128,128]{2,1,0:T(8,128)S(1)} %slice.136), channel_id=1, source_target_pairs={{0,8},{1,9},{2,10},{3,11},{4,12},{5,13},{6,14},{7,15},{8,0},{9,1},... | collective-permute-start | bytes 196616 | tf_op jit(solution)/shard_map/ppermute | solution.py:11
  186.9 3.1 %copy-start.1 = (f32[4096,128]{1,0:T(8,128)S(1)}, f32[4096,128]{1,0:T(8,128)}, u32[]{:S(2)}) copy-start(f32[4096,128]{1,0:T(8,128)} %gather_fusion) | copy-start | bytes 6291460
where the time goes:
time: 228 us; the launch traced here: 227 us
  blocking collectives  90.2 us (40%)
  local copies, waits for them, and re-layouts  49.9 us (22%)
  waiting for transfers between devices  26.8 us (12%)
  other arithmetic  26.7 us (12%)
  matrix products  23.8 us (10%)
  starting transfers between devices  8.49 us (4%)
    psum x2, blocking collectives, squares(): return lax.psum(jnp.sum(values * values, axis=1), 'leaf')  60.8 us
    psum x1, blocking collectives, on_device(): curvature = lax.psum(jnp.sum(direction * image_field, axis=1), 'leaf')  29.5 us
    ppermute x8, waiting for transfers between devices, from_partner(): lax.ppermute(array, axis, [(i, i ^ 1 << stride) for i in range(lax.axis_s...  26.8 us
    gather x2, local copies, waits for them, and re-layouts, on_device(): ordered = jnp.take(right_side, local_order, axis=1)  16.1 us
    unnamed x37, local copies, waits for them, and re-layouts  15.3 us
    scatter x1, other arithmetic, on_device(): field_solution = jnp.zeros_like(solution).at[:, local_order].set(solution)  14.8 us
    scatter x1, local copies, waits for them, and re-layouts, on_device(): field_residual = jnp.zeros_like(residual).at[:, local_order].set(residual)  12.5 us
    dot_general x2, matrix products, apply_operator(): jnp.einsum('nbp,lrbp->blnr', probe_tiles, basis_tiles, preferred_element_...  11.8 us
  transfers between devices with their start and end apart: 8, of which 6 were waited for; matrix products, arithmetic and copies ran while one was open for 4% of the time, Pallas kernels for 0%

commit v1 on v0

--- a/solution.py
+++ b/solution.py
@@ -81,7 +81,9 @@
         image_field = apply_operator(
             direction.astype(jnp.bfloat16), leaf_blocks, bases, rank_weights
         )
-        curvature = lax.psum(jnp.sum(direction * image_field, axis=1), "leaf")
+        curvature = jnp.sum(
+            lax.all_gather(jnp.sum(direction * image_field, axis=1), "leaf"), axis=0
+        )
         step_size = norm_now / curvature
         solution = solution + step_size[:, None] * direction
         residual = residual - step_size[:, None] * image_field

time: 228 us -> 245 us (1.075)
  blocking collectives: 90.2 us -> 101 us
  starting transfers between devices: 8.49 us -> 0.95 us
  matrix products: 23.8 us -> 28.7 us
  local copies, waits for them, and re-layouts: 49.9 us -> 54.7 us
  waiting for transfers between devices: 26.8 us -> 31.2 us
    all_gather x0 -> x2, blocking collectives: none -> 34.6 us  [on_device(): lax.all_gather(jnp.sum(direction * image_field, axis=1), 'leaf')]
    psum x1 -> x0, blocking collectives: 29.5 us -> none  [on_device(): curvature = lax.psum(jnp.sum(direction * image_field, axis=1), 'leaf')]
    ppermute x8, starting transfers between devices: 8.49 us -> 0.95 us  [from_partner(): lax.ppermute(array, axis, [(i, i ^ 1 << stride) for i in range(lax.axis_s...]
    psum x2, blocking collectives: 60.8 us -> 66.5 us  [squares(): return lax.psum(jnp.sum(values * values, axis=1), 'leaf')]
    ppermute x8, waiting for transfers between devices: 26.8 us -> 31.2 us  [from_partner(): lax.ppermute(array, axis, [(i, i ^ 1 << stride) for i in range(lax.axis_s...]
    unnamed x37 -> x35, local copies, waits for them, and re-layouts: 15.3 us -> 19.4 us
    dot_general x2, matrix products: 9.11 us -> 12.7 us  [apply_operator(): jnp.einsum('lbnr,lrbp->nbp', stacked, basis_tiles, preferred_element_type...]
  transfers between devices with their start and end apart: 8 -> 8, of which waited for: 6 -> 6; matrix products, arithmetic and copies ran while one was open for 4% -> 6% of each run, Pallas kernels for 0% -> 0%
where the time goes in v1:
time: 245 us; the launch traced here: 244 us
  blocking collectives  101 us (41%)
  local copies, waits for them, and re-layouts  54.7 us (22%)
  waiting for transfers between devices  31.2 us (13%)
  matrix products  28.7 us (12%)
  other arithmetic  26.8 us (11%)
    psum x2, blocking collectives, squares(): return lax.psum(jnp.sum(values * values, axis=1), 'leaf')  66.5 us
    all_gather x2, blocking collectives, on_device(): lax.all_gather(jnp.sum(direction * image_field, axis=1), 'leaf')  34.6 us
    ppermute x8, waiting for transfers between devices, from_partner(): lax.ppermute(array, axis, [(i, i ^ 1 << stride) for i in range(lax.axis_s...  31.2 us
    unnamed x35, local copies, waits for them, and re-layouts  19.4 us
    gather x2, local copies, waits for them, and re-layouts, on_device(): ordered = jnp.take(right_side, local_order, axis=1)  16.1 us
    scatter x1, other arithmetic, on_device(): field_solution = jnp.zeros_like(solution).at[:, local_order].set(solution)  14.8 us
    dot_general x2, matrix products, apply_operator(): jnp.einsum('lbnr,lrbp->nbp', stacked, basis_tiles, preferred_element_type...  12.7 us
    scatter x1, local copies, waits for them, and re-layouts, on_device(): field_residual = jnp.zeros_like(residual).at[:, local_order].set(residual)  12.5 us
  transfers between devices with their start and end apart: 8, of which 6 were waited for; matrix products, arithmetic and copies ran while one was open for 6% of the time, Pallas kernels for 0%

profile of v1, /device:TPU:0, one launch (start us, length us, event | category | flops | bytes accessed | tf_op | source)
XLA Modules:
  0.0 244.4 jit_solution(6603786406199990851)
XLA Ops:
  0.6 0.7 compare_and_fusion
  1.4 1.9 copy.24
  3.3 14.2 %gather_fusion = f32[4096,128]{1,0:T(8,128)} fusion(f32[128,4096]{0,1:T(8,128)S(1)} %copy.24, s32[4096]{0:T(1024)S(1)} %broadcast_clamp_fusion), kind=kCustom, calls=%fused_computation | custom fusion | bytes 4210688 | tf_op jit(solution)/shard_map/jit(_take)/gather | solution.py:75
  17.5 1.9 copy.25
  19.4 5.5 %fusion.25 = f32[8,7,128,128]{3,2,1,0:T(8,128)S(1)} fusion(bf16[7,16,8,8,512]{4,3,2,1,0:T(8,128)(2,1)} %bitcast.157, f32[128,8,512]{2,0,1:T(8,128)S(1)} %copy.25, pred[8,512]{1,0:T(8,128)(4,1)S(1)} %broadcast_in_dim.46), kind=kOutput, calls=%fused_computation.41 | convolution fusion | flops 940048384 | bytes 13111296 | tf_op jit(solution)/shard_map/nbp,lrbp->blnr/dot_general | solution.py:42
  25.1 0.5 collective-permute-start
  25.6 0.1 slice_reduce_fusion.3
  25.7 0.8 copy-done
  26.6 2.1 multiply_reduce_fusion.3
  28.8 0.8 constant_dynamic-update-slice_fusion.1
  29.7 2.2 fusion.47
  31.9 0.8 constant_dynamic-update-slice_fusion
  32.6 35.0 %psum.14 = f32[128]{0:T(128)S(1)} all-reduce(f32[128]{0:T(128)S(1)} %multiply_reduce_fusion.3), channel_id=1, replica_groups=mesh['groups'=2,'leaf'=16] {'leaf'}, use_global_device_ids=true, to_apply=%region_1.2 | all-reduce | flops 128 | bytes 1024 | tf_op jit(solution)/shard_map/psum | solution.py:68
  67.6 0.7 broadcast_dynamic-update-slice_fusion.9
  68.6 0.7 broadcast_dynamic-update-slice_fusion.8
  69.3 4.9 %collective-permute-done.1 = f32[3,128,128]{2,1,0:T(8,128)S(1)} collective-permute-done((f32[3,128,128]{2,1,0:T(8,128)S(1)}, f32[3,128,128]{2,1,0:T(8,128)S(1)}, u32[]{:S(2)}, u32[]{:S(2)}) %collective-permute-start.1) | collective-permute-done | bytes 196640 | tf_op jit(solution)/shard_map/ppermute | solution.py:11
  74.3 5.4 %collective-permute-done.2 = f32[2,128,128]{2,1,0:T(8,128)S(1)} collective-permute-done((f32[2,128,128]{2,1,0:T(8,128)S(1)}, f32[2,128,128]{2,1,0:T(8,128)S(1)}, u32[]{:S(2)}, u32[]{:S(2)}) %collective-permute-start.2) | collective-permute-done | bytes 131104 | tf_op jit(solution)/shard_map/ppermute | solution.py:11
  79.8 0.7 broadcast_dynamic-update-slice_fusion.7
  80.6 4.4 %collective-permute-done.3 = f32[1,128,128]{2,1,0:T(8,128)S(1)} collective-permute-done((f32[1,128,128]{2,1,0:T(8,128)S(1)}, f32[1,128,128]{2,1,0:T(8,128)S(1)}, u32[]{:S(2)}, u32[]{:S(2)}) %collective-permute-start.3) | collective-permute-done | bytes 65568 | tf_op jit(solution)/shard_map/ppermute | solution.py:11
  85.0 0.7 broadcast_dynamic-update-slice_fusion.6
  85.7 0.7 broadcast_dynamic-update-slice_fusion.5
  86.5 6.4 %multiply_reduce_fusion.2 = (f32[128]{0:T(128)S(1)}, f32[128,8,512]{2,0,1:T(8,128)}) fusion(f32[128,8,512]{2,0,1:T(8,128)S(1)} %copy.25, pred[8,512]{1,0:T(8,128)(4,1)S(1)} %broadcast_in_dim.46, f32[8,128,512]{2,1,0:T(8,128)S(1)} %copy-done.8, bf16[7,8,128,128]{3,2,0,1:T(8,128)(2,1)} %broadcast_dynamic-update-slice_fusion.5, ...), kind=kOutput, calls=%fused_computation.39 | convolution fusion | flops 941621120 | bytes 15471104 | tf_op jit(solution)/shard_map/lbnr,lrbp->nbp/dot_general | solution.py:61
  92.8 17.1 %all-gather.2 = f32[16,1,128]{2,1,0:T(1,128)S(1)} all-gather(f32[1,1,128]{2,1,0:T(1,128)S(1)} %bitcast.171), channel_id=2, replica_groups=mesh['groups'=2,'leaf'=16] {'leaf'}, dimensions={0}, use_global_device_ids=true | all-gather | bytes 8704 | tf_op jit(solution)/shard_map/all_gather | solution.py:85
  110.0 2.1 multiply_reduce_fusion.1
  112.1 31.5 %psum.15 = f32[128]{0:T(128)S(1)} all-reduce(f32[128]{0:T(128)S(1)} %multiply_reduce_fusion.1), channel_id=1, replica_groups=mesh['groups'=2,'leaf'=16] {'leaf'}, use_global_device_ids=true, to_apply=%region_9.10 | all-reduce | flops 128 | bytes 1024 | tf_op jit(solution)/shard_map/psum | solution.py:68
  143.6 2.2 multiply_add_fusion
  145.8 6.3 %fusion.28 = f32[8,7,128,128]{3,2,1,0:T(8,128)S(1)} fusion(bf16[7,16,8,8,512]{4,3,2,1,0:T(8,128)(2,1)} %bitcast.159, f32[128,8,512]{2,0,1:T(8,128)S(1)} %multiply_add_fusion), kind=kOutput, calls=%fused_computation.42 | convolution fusion | flops 940048384 | bytes 13107200 | tf_op jit(solution)/shard_map/nbp,lrbp->blnr/dot_general | solution.py:42
  152.3 2.0 copy-done.6
  154.2 2.0 fusion.45
  156.4 0.7 constant_dynamic-update-slice_fusion.3
  157.2 0.8 constant_dynamic-update-slice_fusion.2
  158.0 1.8 copy.30
  159.8 0.7 broadcast_dynamic-update-slice_fusion.4
  160.7 0.7 broadcast_dynamic-update-slice_fusion.3
  161.5 6.6 %collective-permute-done.5 = f32[3,128,128]{2,1,0:T(8,128)S(1)} collective-permute-done((f32[3,128,128]{2,1,0:T(8,128)S(1)}, f32[3,128,128]{2,1,0:T(8,128)S(1)}, u32[]{:S(2)}, u32[]{:S(2)}) %collective-permute-start.5) | collective-permute-done | bytes 196640 | tf_op jit(solution)/shard_map/ppermute | solution.py:11
  168.2 5.1 %collective-permute-done.6 = f32[2,128,128]{2,1,0:T(8,128)S(1)} collective-permute-done((f32[2,128,128]{2,1,0:T(8,128)S(1)}, f32[2,128,128]{2,1,0:T(8,128)S(1)}, u32[]{:S(2)}, u32[]{:S(2)}) %collective-permute-start.6) | collective-permute-done | bytes 131104 | tf_op jit(solution)/shard_map/ppermute | solution.py:11
  173.4 0.7 broadcast_dynamic-update-slice_fusion.2
  174.1 4.8 %collective-permute-done.7 = f32[1,128,128]{2,1,0:T(8,128)S(1)} collective-permute-done((f32[1,128,128]{2,1,0:T(8,128)S(1)}, f32[1,128,128]{2,1,0:T(8,128)S(1)}, u32[]{:S(2)}, u32[]{:S(2)}) %collective-permute-start.7) | collective-permute-done | bytes 65568 | tf_op jit(solution)/shard_map/ppermute | solution.py:11
  179.0 0.7 broadcast_dynamic-update-slice_fusion.1
  179.7 0.7 broadcast_dynamic-update-slice_fusion
  180.5 6.4 %multiply_reduce_fusion = (f32[128]{0:T(128)S(1)}, f32[128,8,512]{2,0,1:T(8,128)}) fusion(f32[128,8,512]{2,0,1:T(8,128)S(1)} %copy-done.3, f32[8,128,512]{2,1,0:T(8,128)S(1)} %copy-done.7, bf16[7,8,128,128]{3,2,0,1:T(8,128)(2,1)} %broadcast_dynamic-update-slice_fusion, bf16[7,16,8,8,512]{4,3,2,1,0:T(8,128)(2,1)} %bitcast.160), kind=kOutput, calls=%fused_computation.34 | convolution fusion | flops 941096832 | bytes 15467008 | tf_op jit(solution)/shard_map/lbnr,lrbp->nbp/dot_general | solution.py:61
  186.8 17.5 %all-gather.3 = f32[16,1,128]{2,1,0:T(1,128)S(1)} all-gather(f32[1,1,128]{2,1,0:T(1,128)S(1)} %bitcast.170), channel_id=3, replica_groups=mesh['groups'=2,'leaf'=16] {'leaf'}, dimensions={0}, use_global_device_ids=true | all-gather | bytes 8704 | tf_op jit(solution)/shard_map/all_gather | solution.py:85
  204.3 3.1 %copy.31 = f32[128,8,512]{0,2,1:T(8,128)} copy(f32[128,8,512]{2,0,1:T(8,128)} %get-tuple-element.32) | data formatting | bytes 4194304 | tf_op jit(solution)/shard_map/add | solution.py:64
  207.4 3.9 %fusion.14 = (f32[128,4096]{0,1:T(8,128)}, f32[128,4096]{0,1:T(8,128)}) fusion(f32[128,8,512]{0,2,1:T(8,128)} %copy.31, f32[128]{0:T(128)S(1)} %div.11, f32[128,8,512]{0,2,1:T(8,128)} %copy.30, f32[128]{0:T(128)S(1)} %div.9, f32[4096,128]{1,0:T(8,128)S(1)} %copy-done.1, pred[4096]{0:T(1024)(128)(4,1)S(1)} %get-tuple-element.10), kind=kLoop, calls=%fused_computation.20 | loop fusion | flops 2621440 | bytes 10490880 | tf_op jit(solution)/shard_map/sub | solution.py:89
  211.3 12.5 %scatter_custom_fusion.1 = f32[128,4096]{0,1:T(8,128)} fusion(s32[4096]{0:T(1024)S(1)} %get-tuple-element.11, f32[128,4096]{0,1:T(8,128)} %get-tuple-element.8, f32[]{:T(128)} %constant.13.clone.1), kind=kCustom, calls=%fused_computation.17 | custom fusion | bytes 4194308 | tf_op jit(solution)/shard_map/scatter | solution.py:95
  223.8 2.9 %copy.33 = f32[128,4096]{1,0:T(8,128)} copy(f32[128,4096]{0,1:T(8,128)} %scatter_custom_fusion.1) | data formatting | bytes 4194304
  226.7 14.8 %scatter_custom_fusion = f32[128,4096]{0,1:T(8,128)} fusion(s32[4096]{0:T(1024)S(1)} %get-tuple-element.11, f32[128,4096]{0,1:T(8,128)} %get-tuple-element.9, f32[4096,128]{1,0:T(8,128)S(1)} %copy-done.1, f32[128]{0:T(128)S(1)} %div.10, f32[128]{0:T(128)S(1)} %div.11, f32[128]{0:T(128)S(1)} %div.9, f32[]{:T(128)} %constant.18.clone.1, ...), kind=kCustom, calls=%fused_computation.21 | custom fusion | flops 3145728 | bytes 6297096 | tf_op jit(solution)/shard_map/scatter | solution.py:94
  241.5 2.9 %copy.32 = f32[128,4096]{1,0:T(8,128)} copy(f32[128,4096]{0,1:T(8,128)} %scatter_custom_fusion) | data formatting | bytes 4194304
  (70 shorter events, 1.5 us)
Async XLA Ops:
  25.0 1.6 copy-start
  25.1 3.6 %copy-start.9 = (f32[7,128]{1,0:T(8,128)S(1)}, f32[7,128]{1,0:T(8,128)}, u32[]{:S(2)}) copy-start(f32[7,128]{1,0:T(8,128)} %param.9) | copy-start | bytes 10756
  25.1 43.3 %collective-permute-start = (f32[4,128,128]{2,1,0:T(8,128)S(1)}, f32[4,128,128]{2,1,0:T(8,128)S(1)}, u32[]{:S(2)}, u32[]{:S(2)}) collective-permute-start(f32[4,128,128]{2,1,0:T(8,128)S(1)} %slice_reduce_fusion.1), channel_id=1, source_target_pairs={{0,1},{1,0},{2,3},{3,2},{4,5},{5,4},{6,7},{7,6},{8,9},{9,8},{10,11... | collective-permute-start | bytes 786440 | tf_op jit(solution)/shard_map/ppermute | solution.py:11
  26.6 3.1 %copy-start.5 = (bf16[8,512,512]{2,1,0:T(8,128)(2,1)S(1)}, bf16[8,512,512]{2,1,0:T(8,128)(2,1)}, u32[]{:S(2)}) copy-start(bf16[8,512,512]{2,1,0:T(8,128)(2,1)} %param.7) | copy-start | bytes 12582916
  68.4 18.1 %copy-start.8 = (f32[8,128,512]{2,1,0:T(8,128)S(1)}, f32[8,128,512]{2,1,0:T(8,128)}, u32[]{:S(2)}) copy-start(f32[8,128,512]{2,1,0:T(8,128)} %fusion.47) | copy-start | bytes 6291460
  68.5 5.7 %collective-permute-start.1 = (f32[3,128,128]{2,1,0:T(8,128)S(1)}, f32[3,128,128]{2,1,0:T(8,128)S(1)}, u32[]{:S(2)}, u32[]{:S(2)}) collective-permute-start(f32[3,128,128]{2,1,0:T(8,128)S(1)} %slice.122), channel_id=1, source_target_pairs={{0,2},{1,3},{2,0},{3,1},{4,6},{5,7},{6,4},{7,5},{8,10},{9,11},{10,... | collective-permute-start | bytes 589832 | tf_op jit(solution)/shard_map/ppermute | solution.py:11
  74.2 5.5 %collective-permute-start.2 = (f32[2,128,128]{2,1,0:T(8,128)S(1)}, f32[2,128,128]{2,1,0:T(8,128)S(1)}, u32[]{:S(2)}, u32[]{:S(2)}) collective-permute-start(f32[2,128,128]{2,1,0:T(8,128)S(1)} %slice.124), channel_id=1, source_target_pairs={{0,4},{1,5},{2,6},{3,7},{4,0},{5,1},{6,2},{7,3},{8,12},{9,13},{10,... | collective-permute-start | bytes 393224 | tf_op jit(solution)/shard_map/ppermute | solution.py:11
  79.8 5.2 %collective-permute-start.3 = (f32[1,128,128]{2,1,0:T(8,128)S(1)}, f32[1,128,128]{2,1,0:T(8,128)S(1)}, u32[]{:S(2)}, u32[]{:S(2)}) collective-permute-start(f32[1,128,128]{2,1,0:T(8,128)S(1)} %slice.126), channel_id=1, source_target_pairs={{0,8},{1,9},{2,10},{3,11},{4,12},{5,13},{6,14},{7,15},{8,0},{9,1},... | collective-permute-start | bytes 196616 | tf_op jit(solution)/shard_map/ppermute | solution.py:11
  145.8 6.5 %copy-start.2 = (f32[128,8,512]{2,0,1:T(8,128)}, f32[128,8,512]{2,0,1:T(8,128)S(1)}, u32[]{:S(2)}) copy-start(f32[128,8,512]{2,0,1:T(8,128)S(1)} %multiply_add_fusion) | copy-start | bytes 6291460
  152.0 2.2 copy-start.6
  156.3 1.7 copy-start.4
  156.3 4.3 %collective-permute-start.4 = (f32[4,128,128]{2,1,0:T(8,128)S(1)}, f32[4,128,128]{2,1,0:T(8,128)S(1)}, u32[]{:S(2)}, u32[]{:S(2)}) collective-permute-start(f32[4,128,128]{2,1,0:T(8,128)S(1)} %slice_reduce_fusion), channel_id=1, source_target_pairs={{0,1},{1,0},{2,3},{3,2},{4,5},{5,4},{6,7},{7,6},{8,9},{9,8},{10,11... | collective-permute-start | bytes 786440 | tf_op jit(solution)/shard_map/ppermute | solution.py:11
  160.6 19.9 %copy-start.3 = (f32[128,8,512]{2,0,1:T(8,128)S(1)}, f32[128,8,512]{2,0,1:T(8,128)}, u32[]{:S(2)}) copy-start(f32[128,8,512]{2,0,1:T(8,128)} %copy-done.2) | copy-start | bytes 6291460
  160.6 19.9 %copy-start.7 = (f32[8,128,512]{2,1,0:T(8,128)S(1)}, f32[8,128,512]{2,1,0:T(8,128)}, u32[]{:S(2)}) copy-start(f32[8,128,512]{2,1,0:T(8,128)} %fusion.45) | copy-start | bytes 6291460
  160.7 7.4 %collective-permute-start.5 = (f32[3,128,128]{2,1,0:T(8,128)S(1)}, f32[3,128,128]{2,1,0:T(8,128)S(1)}, u32[]{:S(2)}, u32[]{:S(2)}) collective-permute-start(f32[3,128,128]{2,1,0:T(8,128)S(1)} %slice.132), channel_id=1, source_target_pairs={{0,2},{1,3},{2,0},{3,1},{4,6},{5,7},{6,4},{7,5},{8,10},{9,11},{10,... | collective-permute-start | bytes 589832 | tf_op jit(solution)/shard_map/ppermute | solution.py:11
  168.1 5.2 %collective-permute-start.6 = (f32[2,128,128]{2,1,0:T(8,128)S(1)}, f32[2,128,128]{2,1,0:T(8,128)S(1)}, u32[]{:S(2)}, u32[]{:S(2)}) collective-permute-start(f32[2,128,128]{2,1,0:T(8,128)S(1)} %slice.134), channel_id=1, source_target_pairs={{0,4},{1,5},{2,6},{3,7},{4,0},{5,1},{6,2},{7,3},{8,12},{9,13},{10,... | collective-permute-start | bytes 393224 | tf_op jit(solution)/shard_map/ppermute | solution.py:11
  173.3 5.7 %collective-permute-start.7 = (f32[1,128,128]{2,1,0:T(8,128)S(1)}, f32[1,128,128]{2,1,0:T(8,128)S(1)}, u32[]{:S(2)}, u32[]{:S(2)}) collective-permute-start(f32[1,128,128]{2,1,0:T(8,128)S(1)} %slice.136), channel_id=1, source_target_pairs={{0,8},{1,9},{2,10},{3,11},{4,12},{5,13},{6,14},{7,15},{8,0},{9,1},... | collective-permute-start | bytes 196616 | tf_op jit(solution)/shard_map/ppermute | solution.py:11
  204.3 3.1 %copy-start.1 = (f32[4096,128]{1,0:T(8,128)S(1)}, f32[4096,128]{1,0:T(8,128)}, u32[]{:S(2)}) copy-start(f32[4096,128]{1,0:T(8,128)} %gather_fusion) | copy-start | bytes 6291460
